TPU v7x, 32 devices: a whole 2x2x4 slice. The times are simulated.
32 devices in a mesh: grp: 4 (over y, x), col: 8 (over z, core).
Axes of the slice: x: 2, y: 2, z: 4, core: 2. Of those that a mesh axis runs over, the one named last changes fastest.
Arguments:
- blocks: bfloat16 [6144, 32, 1024], P(('grp', 'col'))
- i_index: int32 [6144], P(('grp', 'col')), may hold values from 0 to 15
- j_index: int32 [6144], P(('grp', 'col')), may hold values from 0 to 63
- k_index: int32 [6144], P(('grp', 'col')), may hold values from 0 to 15
- block_count: int32 [32], P(('grp', 'col')), may hold values from 24 to 192, as said below
- b_factor: float32 [16384, 256], P(('grp', 'col'))
- c_factor: float32 [4096, 256], P(('grp', 'col'))
Outputs:
- a_update: float32 [2048, 256], P(('grp', 'col'))
- b_update: float32 [16384, 256], P(('grp', 'col'))
Inputs may be any that keep to these rules, and one draw needn't show every extreme that they name: block_count[d] is the number of live slots of device d = 8 * (grp index) + (col index): its slots d * 192 to d * 192 + block_count[d] - 1; every other slot is ignored. Some device has exactly 192 live slots.
All inputs are finite; a program needn't handle non-finite values.
Results may differ from a plain program's by a relative error of at most 0.005.
The roundings to bfloat16 on the way count: a program that leaves them out, or rounds other values in their place, can miss the bound.
Values may be sent and summed in bfloat16 or wider, within the bound.
A program may use at most 128 MiB of HBM per device.

v0:
```python
import functools
import jax
import jax.numpy as jnp
from jax import lax
from jax.experimental import pallas as pl
from jax.experimental.pallas import tpu as pltpu
from jax.sharding import PartitionSpec as P

HIGHEST = lax.Precision.HIGHEST
GROUP = 16
UNROLL = 4
QUARTER = 32
LANES = 128
VMEM_LIMIT = 56 * 1024 * 1024


def khatri_rao(left, tail, first):
    rows = [
        jnp.broadcast_to(left[first + t : first + t + 1, :], tail.shape).astype(jnp.bfloat16) * tail
        for t in range(8)
    ]
    return jnp.concatenate(rows, axis=0)


def product_rows(lhs_part, left, tail):
    total = None
    for q in range(4):
        term = jnp.dot(
            lhs_part(q), khatri_rao(left, tail, 8 * q), preferred_element_type=jnp.float32
        )
        total = term if total is None else total + term
    return total


def slot_loop(count, do_slot):
    base = pl.program_id(0) * GROUP
    steps = jnp.clip((count - base + UNROLL - 1) // UNROLL, 0, GROUP // UNROLL)

    def body(step, carry):
        for u in range(UNROLL):
            local = step * UNROLL + u
            do_slot(local, base + local, u)
        return carry

    lax.fori_loop(0, steps, body, 0)


def mode_one_kernel(i_ref, j_ref, k_ref, n_ref, x_ref, b_ref, c_ref, out_ref):
    @pl.when(pl.program_id(0) == 0)
    def _():
        out_ref[...] = jnp.zeros_like(out_ref)

    count = n_ref[0]

    def do_slot(local, slot, u):
        left = b_ref[pl.ds(pl.multiple_of(j_ref[slot] * 32, 32), 32), :].astype(jnp.float32)
        tail = c_ref[pl.ds(pl.multiple_of(k_ref[slot] * 32, 32), 32), :]
        result = product_rows(lambda q: x_ref[local, :, q * 256 : (q + 1) * 256], left, tail)
        alive = (slot < count).astype(jnp.float32)
        rows = pl.ds(pl.multiple_of(i_ref[slot] * 32, 32), 32)
        out_ref[rows, :] += result * alive

    slot_loop(count, do_slot)


def quarter_swap(parts):
    lane = lax.broadcasted_iota(jnp.int32, parts[0].shape, 1)
    even = (lane // QUARTER) % 2 == 0
    low = lane < 2 * QUARTER

    def pair(p, q, keep, dist):
        return (
            jnp.where(keep, p, pltpu.roll(q, dist, 1)),
            jnp.where(keep, pltpu.roll(p, LANES - dist, 1), q),
        )

    p0, p1 = pair(parts[0], parts[1], even, QUARTER)
    p2, p3 = pair(parts[2], parts[3], even, QUARTER)
    r0, r2 = pair(p0, p2, low, 2 * QUARTER)
    r1, r3 = pair(p1, p3, low, 2 * QUARTER)
    return [r0, r1, r2, r3]


def mode_two_kernel(i_ref, j_ref, k_ref, n_ref, x_ref, a_ref, c_ref, out_ref, wide):
    @pl.when(pl.program_id(0) == 0)
    def _():
        out_ref[...] = jnp.zeros_like(out_ref)

    count = n_ref[0]

    def do_slot(local, slot, u):
        for col in range(8):
            wide[u, 32 * col : 32 * col + 32, :] = x_ref[
                local, :, col * LANES : (col + 1) * LANES
            ].astype(jnp.float32)

        def lhs_part(q):
            pieces = []
            for half in range(2):
                first = q * 8 + half * 4
                parts = [wide[u, pl.ds(first + t, 8, stride=32), :] for t in range(4)]
                pieces.append(jnp.concatenate(quarter_swap(parts), axis=0).astype(jnp.bfloat16))
            return jnp.concatenate(pieces, axis=1)

        left = a_ref[pl.ds(pl.multiple_of(i_ref[slot] * 32, 32), 32), :].astype(jnp.float32)
        tail = c_ref[pl.ds(pl.multiple_of(k_ref[slot] * 32, 32), 32), :]
        result = product_rows(lhs_part, left, tail)
        alive = (slot < count).astype(jnp.float32)
        rows = pl.ds(pl.multiple_of(j_ref[slot] * 32, 32), 32)
        out_ref[rows, :] += result * alive

    slot_loop(count, do_slot)


def mode_call(kernel, scalars, blocks, left, tail, rows, scratch):
    slots, edge, width = blocks.shape
    rank = left.shape[1]
    grid_spec = pltpu.PrefetchScalarGridSpec(
        num_scalar_prefetch=4,
        grid=(slots // GROUP,),
        in_specs=[
            pl.BlockSpec((GROUP, edge, width), lambda g, *_: (g, 0, 0)),
            pl.BlockSpec(left.shape, lambda g, *_: (0, 0)),
            pl.BlockSpec(tail.shape, lambda g, *_: (0, 0)),
        ],
        out_specs=pl.BlockSpec((rows, rank), lambda g, *_: (0, 0)),
        scratch_shapes=scratch,
    )
    return pl.pallas_call(
        kernel,
        grid_spec=grid_spec,
        out_shape=jax.ShapeDtypeStruct((rows, rank), jnp.float32),
        compiler_params=pltpu.CompilerParams(vmem_limit_bytes=VMEM_LIMIT),
        cost_estimate=pl.CostEstimate(
            flops=2 * slots * edge * width * rank,
            bytes_accessed=2 * slots * edge * width,
            transcendentals=0,
        ),
    )(*scalars, blocks, left, tail)


def inverse_kernel(g_ref, out_ref):
    gram = g_ref[...]
    row = lax.broadcasted_iota(jnp.int32, gram.shape, 0)
    col = lax.broadcasted_iota(jnp.int32, gram.shape, 1)
    eye = (row == col).astype(jnp.float32)
    scale_row = lax.rsqrt(jnp.sum(gram * eye, axis=0, keepdims=True))
    scale_col = lax.rsqrt(jnp.sum(gram * eye, axis=1, keepdims=True))
    unit = gram * scale_row * scale_col
    bound = 1.0 / jnp.max(jnp.sum(jnp.abs(unit), axis=0, keepdims=True))

    def residual(x):
        return eye - jnp.dot(unit, x, precision=HIGHEST, preferred_element_type=jnp.float32)

    def update(x, r):
        return x + jnp.dot(x, r, precision=HIGHEST, preferred_element_type=jnp.float32)

    unit_low = unit.astype(jnp.bfloat16)

    def body_low(state):
        step, _, x, r = state
        x = x + jnp.dot(
            x.astype(jnp.bfloat16), r.astype(jnp.bfloat16), preferred_element_type=jnp.float32
        )
        r = eye - jnp.dot(unit_low, x.astype(jnp.bfloat16), preferred_element_type=jnp.float32)
        return step + 1, jnp.sum(r * r), x, r

    def body(state):
        step, _, x, r = state
        x = update(x, r)
        r = residual(x)
        return step + 1, jnp.sum(r * r), x, r

    def more_low(state):
        return jnp.logical_and(state[0] < 16, state[1] > 0.01)

    def more(state):
        return jnp.logical_and(state[0] < 60, state[1] > 1e-6)

    start = eye * bound
    start_r = eye - unit * bound
    _, _, x, _ = lax.while_loop(
        more_low, body_low, (jnp.int32(0), jnp.sum(start_r * start_r), start, start_r)
    )
    r = residual(x)
    good = jnp.sum(r * r) < 0.25
    x = jnp.where(good, x, start)
    r = jnp.where(good, r, start_r)
    _, _, x, r = lax.while_loop(more, body, (jnp.int32(0), jnp.sum(r * r), x, r))
    out_ref[...] = update(x, r) * scale_row * scale_col


def inverse(gram):
    return pl.pallas_call(
        inverse_kernel,
        out_shape=jax.ShapeDtypeStruct(gram.shape, jnp.float32),
        in_specs=[pl.BlockSpec(memory_space=pltpu.VMEM)],
        out_specs=pl.BlockSpec(memory_space=pltpu.VMEM),
        compiler_params=pltpu.CompilerParams(vmem_limit_bytes=VMEM_LIMIT),
    )(gram)


def me_of(shape):
    return lax.axis_index("grp"), lax.axis_index("col")


def bits_of(size):
    count = size.bit_length() - 1
    assert size == 1 << count
    return count


def flip(position, mask):
    out = position
    for t in range(mask.bit_length()):
        if (mask >> t) & 1:
            bit = (position // (1 << t)) % 2
            out = out + (1 - 2 * bit) * (1 << t)
    return out


def greet(targets):
    barrier = pltpu.get_barrier_semaphore()
    for target in targets:
        pl.semaphore_signal(barrier, inc=1, device_id=target, device_id_type=pl.DeviceIdType.MESH)
    pl.semaphore_wait(barrier, len(targets))


def send(src, dst, sems, index, target):
    copy = pltpu.make_async_remote_copy(
        src_ref=src,
        dst_ref=dst,
        send_sem=sems[0].at[index],
        recv_sem=sems[1].at[index],
        device_id=target,
        device_id_type=pl.DeviceIdType.MESH,
    )
    copy.start()
    return copy


def rows_at(first, size):
    return pl.ds(pl.multiple_of(first, 8), size)


def scatter_sum(group, acc, landing, sems, first, offset, rows):
    index, targets = group
    size = len(targets) + 1
    chunk = rows // size
    copies = []
    for number, (other, target) in enumerate(targets):
        place = landing.at[pl.ds(rows - (number + 1) * chunk, chunk), :]
        copies.append(
            send(acc.at[rows_at(offset + other * chunk, chunk), :], place, sems, first + number, target)
        )
    offset = offset + index * chunk
    for number, copy in enumerate(copies):
        copy.wait()
        low = rows - (number + 1) * chunk
        acc[rows_at(offset, chunk), :] += landing[low : low + chunk, :]
    return offset, chunk


def spread(group, full, sems, first, offset, rows):
    index, targets = group
    copies = []
    mine = full.at[rows_at(offset, rows), :]
    for number, (_, target) in enumerate(targets):
        copies.append(send(mine, mine, sems, first + number, target))
    for copy in copies:
        copy.wait()
    return offset - index * rows, rows * (len(targets) + 1)


def scatter_all(groups, acc, landing, sems):
    offset, rows, first = jnp.int32(0), acc.shape[0], 0
    for group in groups:
        offset, rows = scatter_sum(group, acc, landing, sems, first, offset, rows)
        first += len(group[1])
    return offset, rows


def spread_all(groups, full, sems, offset, rows):
    first = sum(len(group[1]) for group in groups)
    for group in reversed(groups):
        offset, rows = spread(group, full, sems, first, offset, rows)
        first += len(group[1])


def core_group():
    g, c = lax.axis_index("grp"), lax.axis_index("col")
    core = lax.rem(c, 2)
    return core, [(1 - core, (g, c + 1 - 2 * core))]


def chip_group(col):
    g, c = lax.axis_index("grp"), lax.axis_index("col")
    chips, core, chip = col // 2, lax.rem(c, 2), c // 2
    others = [lax.rem(chip + p, chips) for p in range(1, chips)]
    return chip, [(other, (g, other * 2 + core)) for other in others]


def grp_group(grp):
    g, c = lax.axis_index("grp"), lax.axis_index("col")
    others = [lax.rem(g + p, grp) for p in range(1, grp)]
    return g, [(other, (other, c)) for other in others]


def grp_stages(size):
    g, c = me_of(size)
    return [((g // (1 << t)) % 2, (flip(g, 1 << t), c)) for t in range(bits_of(size))]


def targets_of(groups):
    return [target for _, targets in groups for _, target in targets]


def square(x):
    high = x.astype(jnp.bfloat16)
    low = (x - high.astype(jnp.float32)).astype(jnp.bfloat16)

    def dot(p, q):
        return lax.dot_general(
            p, q, (((0,), (0,)), ((), ())), preferred_element_type=jnp.float32
        )

    cross = dot(high, low)
    return dot(high, high) + (cross + cross.T)


def gather_kernel(
    grp, col, b_ref, c_ref, b_out, c_out, product_out, third_out, acc, landing, full, *sems
):
    g, c = me_of(grp)
    rank = b_ref.shape[1]
    groups = [core_group(), chip_group(col), grp_group(grp)]
    others = targets_of(groups[2:])
    greet(targets_of(groups))
    pending = []
    for which, (src, out) in enumerate(((c_ref, c_out), (b_ref, b_out))):
        size = src.shape[0]
        mine = out.at[rows_at(g * size, size), :]
        mine[...] = src[...].astype(jnp.bfloat16)
        for number, target in enumerate(others):
            pending.append(send(mine, mine, sems[2:], which * (grp - 1) + number, target))
    for which, src in enumerate((b_ref, c_ref)):
        gram = square(src[...])
        for part in range(rank // LANES):
            first = (which * (rank // LANES) + part) * rank
            acc[first : first + rank, :] = gram[:, part * LANES : (part + 1) * LANES]
    offset, rows = scatter_all(groups, acc, landing, sems)
    full[rows_at(offset, rows), :] = acc[rows_at(offset, rows), :]
    spread_all(groups, full, sems, offset, rows)
    half = acc.shape[0] // 2
    for part in range(rank // LANES):
        second = full[part * rank : (part + 1) * rank, :]
        third = full[half + part * rank : half + (part + 1) * rank, :]
        product_out[:, part * LANES : (part + 1) * LANES] = second * third
        third_out[:, part * LANES : (part + 1) * LANES] = third
    for copy in pending:
        copy.wait()


def first_factor_kernel(
    grp, col, part_ref, inverse_ref, third_ref, update_out, low_out, two_out,
    acc, landing, full, gram, piece, whole, *sems,
):
    g, c = me_of(grp)
    total = part_ref.shape[0]
    own = total // col
    groups = [core_group(), chip_group(col)]
    others = targets_of([grp_group(grp)])
    greet(others + targets_of(groups))
    for block in range(col):
        spot = (block % 2 * (col // 2) + block // 2) * own
        acc[spot : spot + own, :] = part_ref[block * own : (block + 1) * own, :]
    offset, rows = scatter_all(groups, acc, landing, sems)
    update = jnp.dot(
        acc[rows_at(offset, rows), :],
        inverse_ref[...],
        precision=HIGHEST,
        preferred_element_type=jnp.float32,
    )
    update_out[...] = update
    full[rows_at(offset, rows), :] = update
    spread_all(groups, full, sems, offset, rows)
    gram[...] = square(full[...])
    size = gram.shape[0] // grp
    copies = []
    for number, target in enumerate(others):
        copies.append(
            send(gram.at[rows_at(target[0] * size, size), :], piece.at[number], sems[2:], number, target)
        )
    mine = gram[rows_at(g * size, size), :]
    for number, copy in enumerate(copies):
        copy.wait()
        mine = mine + piece[number]
    spot = whole.at[rows_at(g * size, size), :]
    spot[...] = mine
    copies = [
        send(spot, spot, sems[2:], grp - 1 + number, target) for number, target in enumerate(others)
    ]
    for copy in copies:
        copy.wait()
    gram_first = whole[...]
    row = lax.broadcasted_iota(jnp.int32, gram_first.shape, 0)
    column = lax.broadcasted_iota(jnp.int32, gram_first.shape, 1)
    diagonal = jnp.where(row == column, gram_first, 0.0)
    norm_row = jnp.sqrt(jnp.sum(diagonal, axis=0, keepdims=True) + 1e-06)
    norm_col = jnp.sqrt(jnp.sum(diagonal, axis=1, keepdims=True) + 1e-06)
    two_out[...] = gram_first / (norm_col * norm_row) * third_ref[...]
    for block in range(col):
        first = (block % 2 * (col // 2) + block // 2) * own
        low_out[block * own : (block + 1) * own, :] = (
            full[first : first + own, :] / norm_row
        ).astype(jnp.bfloat16)


def second_factor_kernel(grp, part_ref, inverse_ref, out_ref, landing, *sems):
    g, c = me_of(grp)
    count = bits_of(grp)
    own = part_ref.shape[0] // grp
    greet([target for _, target in grp_stages(grp)])
    half = part_ref.shape[1] // 2
    holding = []
    for h in range(2):
        lanes = slice(h * half, (h + 1) * half)
        holding.append(
            {m: part_ref.at[rows_at(flip(g, m) * own, own), lanes] for m in range(grp)}
        )
    spare = [0, 0]
    used = 0
    for stage in range(count):
        copies = []
        for h in range(2):
            bit = stage if h == 0 else count - 1 - stage
            target = (flip(g, 1 << bit), c)
            for m in sorted(holding[h]):
                if not (m >> bit) & 1:
                    place = landing.at[h, spare[h]]
                    spare[h] += 1
                    source = holding[h][m | (1 << bit)]
                    copies.append((h, m, bit, place, send(source, place, sems, used, target)))
                    used += 1
        for h, m, bit, place, copy in copies:
            copy.wait()
            place[...] += holding[h][m][...]
            holding[h][m] = place
            del holding[h][m | (1 << bit)]
    for h in range(2):
        out_ref[:, h * half : (h + 1) * half] = holding[h][0][...]
    rank = out_ref.shape[1]
    solved = jnp.dot(
        out_ref[...], inverse_ref[...], precision=HIGHEST, preferred_element_type=jnp.float32
    )
    out_ref[...] = solved.reshape(own // 32, 4, 8, rank).swapaxes(1, 2).reshape(own, rank)


def remote_call(kernel, number, args, outs, scratch):
    vmem = pl.BlockSpec(memory_space=pltpu.VMEM)
    return pl.pallas_call(
        kernel,
        out_shape=[jax.ShapeDtypeStruct(shape, dtype) for shape, dtype in outs],
        in_specs=[vmem] * len(args),
        out_specs=[vmem] * len(outs),
        scratch_shapes=scratch,
        compiler_params=pltpu.CompilerParams(
            collective_id=number, has_side_effects=True, vmem_limit_bytes=VMEM_LIMIT
        ),
    )(*args)


def semaphores(count):
    return [pltpu.SemaphoreType.DMA((count,))] * 2


def on_device(blocks, i_index, j_index, k_index, block_count, b_factor, c_factor):
    edge = blocks.shape[1]
    rank = b_factor.shape[1]
    grp, col = lax.axis_size("grp"), lax.axis_size("col")
    col_links = col // 2
    f32, bf16 = jnp.float32, jnp.bfloat16
    gram_rows = 2 * rank * (rank // LANES)
    b_range, c_range, gram_one, gram_third = remote_call(
        functools.partial(gather_kernel, grp, col),
        0,
        (b_factor, c_factor),
        [
            ((grp * b_factor.shape[0], rank), bf16),
            ((grp * c_factor.shape[0], rank), bf16),
            ((rank, rank), f32),
            ((rank, rank), f32),
        ],
        [
            pltpu.VMEM((gram_rows, LANES), f32),
            pltpu.VMEM((gram_rows, LANES), f32),
            pltpu.VMEM((gram_rows, LANES), f32),
        ]
        + semaphores(2 * (col_links + grp - 1))
        + semaphores(2 * (grp - 1)),
    )
    scalars = (i_index, j_index, k_index, block_count)
    own_rows = 2 * edge
    first_rows = own_rows * col
    partial_one = mode_call(mode_one_kernel, scalars, blocks, b_range, c_range, first_rows, [])
    a_update, a_range, gram_two = remote_call(
        functools.partial(first_factor_kernel, grp, col),
        1,
        (partial_one, inverse(gram_one), gram_third),
        [((own_rows, rank), f32), ((first_rows, rank), bf16), ((rank, rank), f32)],
        [
            pltpu.VMEM((first_rows, rank), f32),
            pltpu.VMEM((first_rows, rank), f32),
            pltpu.VMEM((first_rows, rank), f32),
            pltpu.VMEM((rank, rank), f32),
            pltpu.VMEM((grp - 1, rank // grp, rank), f32),
            pltpu.VMEM((rank, rank), f32),
        ]
        + semaphores(2 * col_links)
        + semaphores(2 * (grp - 1)),
    )
    inverse_two = inverse(gram_two)
    second_rows = b_range.shape[0]
    partial_two = mode_call(
        mode_two_kernel,
        scalars,
        blocks,
        a_range,
        c_range,
        second_rows,
        [pltpu.VMEM((UNROLL, 8 * edge, LANES), f32)],
    )
    (b_update,) = remote_call(
        functools.partial(second_factor_kernel, grp),
        2,
        (partial_two, inverse_two),
        [((second_rows // grp, rank), f32)],
        [pltpu.VMEM((2, grp - 1, second_rows // grp, rank // 2), f32)] + semaphores(2 * (grp - 1)),
    )
    return (a_update, b_update)


def solution(mesh):
    return jax.shard_map(
        on_device,
        mesh=mesh,
        in_specs=(
            P(("grp", "col"), None, None),
            P(("grp", "col")),
            P(("grp", "col")),
            P(("grp", "col")),
            P(("grp", "col")),
            P(("grp", "col"), None),
            P(("grp", "col"), None),
        ),
        out_specs=(P(("grp", "col"), None), P(("grp", "col"), None)),
        check_vma=False,
    )
```

profile of v0, /device:TPU:17, one launch (start us, length us, event | category | flops | bytes accessed | tf_op | source)
XLA Modules:
  0.0 160.5 jit_solution(951994339736500715)
XLA Ops:
  1.3 32.3 %shard_map.86 = (bf16[2048,256]{1,0:T(8,128)(2,1)}, bf16[512,256]{1,0:T(8,128)(2,1)}, f32[256,256]{1,0:T(8,128)}, f32[256,256]{1,0:T(8,128)}) custom-call(f32[512,256]{1,0:T(8,128)} %b_ref.1, f32[128,256]{1,0:T(8,128)} %c_ref.1), custom_call_target="tpu_custom_call" | custom-call | tf_op jit(solution)/shard_map/pallas_call | solution.py:461
  33.6 26.4 %shard_map.87.part_ref = f32[512,256]{1,0:T(8,128)} custom-call(s32[192]{0:T(256)} %i_ref.3, s32[192]{0:T(256)} %j_ref.3, s32[192]{0:T(256)} %k_ref.3, s32[1]{0:T(128)S(6)} %copy.11.n_ref, bf16[192,32,1024]{2,1,0:T(8,128)(2,1)} %x_ref.3, bf16[2048,256]{1,0:T(8,128)(2,1)} %get-tuple-element.9.b_ref, bf16[512,256]{1,0:T(8,128)(2,1)} %get-tuple-element.10.c_ref), custom_call_target="tpu_custom_call" | custom-call | flops 3221225472 | bytes 12582912 | tf_op jit(solution)/shard_map/pallas_call | solution.py:129
  60.0 8.4 %shard_map.88.inverse_ref = f32[256,256]{1,0:T(8,128)} custom-call(f32[256,256]{1,0:T(8,128)} %get-tuple-element.11.g_ref), custom_call_target="tpu_custom_call" | custom-call | tf_op jit(solution)/shard_map/pallas_call | solution.py:194
  68.4 27.6 %shard_map.89 = (f32[64,256]{1,0:T(8,128)}, bf16[512,256]{1,0:T(8,128)(2,1)}, f32[256,256]{1,0:T(8,128)}) custom-call(f32[512,256]{1,0:T(8,128)} %shard_map.87.part_ref, f32[256,256]{1,0:T(8,128)} %shard_map.88.inverse_ref, f32[256,256]{1,0:T(8,128)} %get-tuple-element.12.third_ref), custom_call_target="tpu_custom_call" | custom-call | tf_op jit(solution)/shard_map/pallas_call | solution.py:461
  96.1 0.0 copy-start
  96.1 6.8 %shard_map.91.inverse_ref = f32[256,256]{1,0:T(8,128)} custom-call(f32[256,256]{1,0:T(8,128)} %get-tuple-element.15.g_ref), custom_call_target="tpu_custom_call" | custom-call | tf_op jit(solution)/shard_map/pallas_call | solution.py:194
  102.9 40.2 %shard_map.90.part_ref = f32[2048,256]{1,0:T(8,128)} custom-call(s32[192]{0:T(256)} %i_ref.3, s32[192]{0:T(256)} %j_ref.3, s32[192]{0:T(256)} %k_ref.3, s32[1]{0:T(128)S(6)} %copy.11.n_ref, bf16[192,32,1024]{2,1,0:T(8,128)(2,1)} %x_ref.3, bf16[512,256]{1,0:T(8,128)(2,1)} %get-tuple-element.14.a_ref, bf16[512,256]{1,0:T(8,128)(2,1)} %get-tuple-element.10.c_ref), custom_call_target="tpu_custom_call" | custom-call | flops 3221225472 | bytes 12582912 | tf_op jit(solution)/shard_map/pallas_call | solution.py:129
  143.0 15.0 %shard_map.92 = f32[512,256]{1,0:T(8,128)} custom-call(f32[2048,256]{1,0:T(8,128)} %shard_map.90.part_ref, f32[256,256]{1,0:T(8,128)} %shard_map.91.inverse_ref), custom_call_target="tpu_custom_call" | custom-call | tf_op jit(solution)/shard_map/pallas_call | solution.py:461
  158.0 0.0 copy-done
  158.0 0.6 copy.12
  158.6 1.9 %copy.13 = f32[512,256]{1,0:T(8,128)} copy(f32[512,256]{1,0:T(8,128)} %shard_map.92) | data formatting | bytes 1048576
Async XLA Ops:
  96.1 61.9 %copy-start = (f32[64,256]{1,0:T(8,128)S(1)}, f32[64,256]{1,0:T(8,128)}, u32[]{:S(2)}) copy-start(f32[64,256]{1,0:T(8,128)} %get-tuple-element.18) | copy-start | bytes 196612
where the time goes:
time: 161 us
  Pallas kernels  157 us (98%)
  local copies, waits for them, and re-layouts  2.5 us (2%)
    pallas_call x3, Pallas kernels, remote_call(): pl.pallas_call(kernel, out_shape=[jax.ShapeDtypeStruct(shape, dtype) for...  74.9 us
    pallas_call x2, Pallas kernels, mode_call(): pl.pallas_call(kernel, grid_spec=grid_spec, out_shape=jax.ShapeDtypeStruc...  66.6 us
    pallas_call x2, Pallas kernels, inverse(): pl.pallas_call(inverse_kernel, out_shape=jax.ShapeDtypeStruct(gram.shape,...  15.2 us

commit v1 on v0

--- a/solution.py
+++ b/solution.py
@@ -8,7 +8,7 @@
 
 HIGHEST = lax.Precision.HIGHEST
 GROUP = 16
-UNROLL = 4
+UNROLL = 8
 QUARTER = 32
 LANES = 128
 VMEM_LIMIT = 56 * 1024 * 1024
@@ -139,8 +139,17 @@
     )(*scalars, blocks, left, tail)
 
 
-def inverse_kernel(g_ref, out_ref):
-    gram = g_ref[...]
+def inverse_kernel(lead_ref, g_ref, out_ref):
+    @pl.when(lead_ref[0] == 0)
+    def _():
+        out_ref[...] = jnp.zeros_like(out_ref)
+
+    @pl.when(lead_ref[0] != 0)
+    def _():
+        out_ref[...] = newton_inverse(g_ref[...])
+
+
+def newton_inverse(gram):
     row = lax.broadcasted_iota(jnp.int32, gram.shape, 0)
     col = lax.broadcasted_iota(jnp.int32, gram.shape, 1)
     eye = (row == col).astype(jnp.float32)
@@ -187,17 +196,31 @@
     x = jnp.where(good, x, start)
     r = jnp.where(good, r, start_r)
     _, _, x, r = lax.while_loop(more, body, (jnp.int32(0), jnp.sum(r * r), x, r))
-    out_ref[...] = update(x, r) * scale_row * scale_col
-
-
-def inverse(gram):
+    return update(x, r) * scale_row * scale_col
+
+
+def inverse(lead, gram):
     return pl.pallas_call(
         inverse_kernel,
         out_shape=jax.ShapeDtypeStruct(gram.shape, jnp.float32),
-        in_specs=[pl.BlockSpec(memory_space=pltpu.VMEM)],
+        in_specs=[
+            pl.BlockSpec(memory_space=pltpu.SMEM),
+            pl.BlockSpec(memory_space=pltpu.VMEM),
+        ],
         out_specs=pl.BlockSpec(memory_space=pltpu.VMEM),
         compiler_params=pltpu.CompilerParams(vmem_limit_bytes=VMEM_LIMIT),
-    )(gram)
+    )(lead, gram)
+
+
+def solve_kernel(sum_ref, mine_ref, other_ref, out_ref):
+    own, rank = sum_ref.shape
+    solved = jnp.dot(
+        sum_ref[...],
+        mine_ref[...] + other_ref[...],
+        precision=HIGHEST,
+        preferred_element_type=jnp.float32,
+    )
+    out_ref[...] = solved.reshape(own // 32, 4, 8, rank).swapaxes(1, 2).reshape(own, rank)
 
 
 def me_of(shape):
@@ -329,14 +352,15 @@
 
 
 def gather_kernel(
-    grp, col, b_ref, c_ref, b_out, c_out, product_out, third_out, acc, landing, full, *sems
+    grp, col, b_ref, c_ref, n_ref, b_out, c_out, product_out, third_out, n_out,
+    acc, landing, full, *sems,
 ):
     g, c = me_of(grp)
     rank = b_ref.shape[1]
     groups = [core_group(), chip_group(col), grp_group(grp)]
     others = targets_of(groups[2:])
     greet(targets_of(groups))
-    pending = []
+    pending = [send(n_ref, n_out, sems[4:], 0, groups[0][1][0][1])]
     for which, (src, out) in enumerate(((c_ref, c_out), (b_ref, b_out))):
         size = src.shape[0]
         mine = out.at[rows_at(g * size, size), :]
@@ -363,7 +387,7 @@
 
 def first_factor_kernel(
     grp, col, part_ref, inverse_ref, third_ref, update_out, low_out, two_out,
-    acc, landing, full, gram, piece, whole, *sems,
+    acc, landing, full, gram, piece, whole, other_inverse, *sems,
 ):
     g, c = me_of(grp)
     total = part_ref.shape[0]
@@ -371,13 +395,15 @@
     groups = [core_group(), chip_group(col)]
     others = targets_of([grp_group(grp)])
     greet(others + targets_of(groups))
+    given = send(inverse_ref, other_inverse, sems[4:], 0, groups[0][1][0][1])
     for block in range(col):
         spot = (block % 2 * (col // 2) + block // 2) * own
         acc[spot : spot + own, :] = part_ref[block * own : (block + 1) * own, :]
     offset, rows = scatter_all(groups, acc, landing, sems)
+    given.wait()
     update = jnp.dot(
         acc[rows_at(offset, rows), :],
-        inverse_ref[...],
+        inverse_ref[...] + other_inverse[...],
         precision=HIGHEST,
         preferred_element_type=jnp.float32,
     )
@@ -416,11 +442,13 @@
         ).astype(jnp.bfloat16)
 
 
-def second_factor_kernel(grp, part_ref, inverse_ref, out_ref, landing, *sems):
+def second_factor_kernel(grp, part_ref, inverse_ref, out_ref, other_out, landing, *sems):
     g, c = me_of(grp)
     count = bits_of(grp)
     own = part_ref.shape[0] // grp
-    greet([target for _, target in grp_stages(grp)])
+    twin = core_group()[1][0][1]
+    greet([target for _, target in grp_stages(grp)] + [twin])
+    given = send(inverse_ref, other_out, sems[2:], 0, twin)
     half = part_ref.shape[1] // 2
     holding = []
     for h in range(2):
@@ -449,11 +477,7 @@
             del holding[h][m | (1 << bit)]
     for h in range(2):
         out_ref[:, h * half : (h + 1) * half] = holding[h][0][...]
-    rank = out_ref.shape[1]
-    solved = jnp.dot(
-        out_ref[...], inverse_ref[...], precision=HIGHEST, preferred_element_type=jnp.float32
-    )
-    out_ref[...] = solved.reshape(own // 32, 4, 8, rank).swapaxes(1, 2).reshape(own, rank)
+    given.wait()
 
 
 def remote_call(kernel, number, args, outs, scratch):
@@ -481,15 +505,16 @@
     col_links = col // 2
     f32, bf16 = jnp.float32, jnp.bfloat16
     gram_rows = 2 * rank * (rank // LANES)
-    b_range, c_range, gram_one, gram_third = remote_call(
+    b_range, c_range, gram_one, gram_third, twin_count = remote_call(
         functools.partial(gather_kernel, grp, col),
         0,
-        (b_factor, c_factor),
+        (b_factor, c_factor, jnp.broadcast_to(block_count.astype(f32), (8, LANES))),
         [
             ((grp * b_factor.shape[0], rank), bf16),
             ((grp * c_factor.shape[0], rank), bf16),
             ((rank, rank), f32),
             ((rank, rank), f32),
+            ((8, LANES), f32),
         ],
         [
             pltpu.VMEM((gram_rows, LANES), f32),
@@ -497,8 +522,12 @@
             pltpu.VMEM((gram_rows, LANES), f32),
         ]
         + semaphores(2 * (col_links + grp - 1))
-        + semaphores(2 * (grp - 1)),
-    )
+        + semaphores(2 * (grp - 1))
+        + semaphores(1),
+    )
+    twin = twin_count[0, :1].astype(jnp.int32)
+    core = lax.axis_index("col") % 2
+    lead = jnp.where(block_count == twin, core == 0, block_count < twin).astype(jnp.int32)
     scalars = (i_index, j_index, k_index, block_count)
     own_rows = 2 * edge
     first_rows = own_rows * col
@@ -506,7 +535,7 @@
     a_update, a_range, gram_two = remote_call(
         functools.partial(first_factor_kernel, grp, col),
         1,
-        (partial_one, inverse(gram_one), gram_third),
+        (partial_one, inverse(lead, gram_one), gram_third),
         [((own_rows, rank), f32), ((first_rows, rank), bf16), ((rank, rank), f32)],
         [
             pltpu.VMEM((first_rows, rank), f32),
@@ -515,11 +544,13 @@
             pltpu.VMEM((rank, rank), f32),
             pltpu.VMEM((grp - 1, rank // grp, rank), f32),
             pltpu.VMEM((rank, rank), f32),
+            pltpu.VMEM((rank, rank), f32),
         ]
         + semaphores(2 * col_links)
-        + semaphores(2 * (grp - 1)),
-    )
-    inverse_two = inverse(gram_two)
+        + semaphores(2 * (grp - 1))
+        + semaphores(1),
+    )
+    inverse_two = inverse(lead, gram_two)
     second_rows = b_range.shape[0]
     partial_two = mode_call(
         mode_two_kernel,
@@ -530,13 +561,22 @@
         second_rows,
         [pltpu.VMEM((UNROLL, 8 * edge, LANES), f32)],
     )
-    (b_update,) = remote_call(
+    own_sum, twin_inverse = remote_call(
         functools.partial(second_factor_kernel, grp),
         2,
         (partial_two, inverse_two),
-        [((second_rows // grp, rank), f32)],
-        [pltpu.VMEM((2, grp - 1, second_rows // grp, rank // 2), f32)] + semaphores(2 * (grp - 1)),
-    )
+        [((second_rows // grp, rank), f32), ((rank, rank), f32)],
+        [pltpu.VMEM((2, grp - 1, second_rows // grp, rank // 2), f32)]
+        + semaphores(2 * (grp - 1))
+        + semaphores(1),
+    )
+    b_update = pl.pallas_call(
+        solve_kernel,
+        out_shape=jax.ShapeDtypeStruct(own_sum.shape, f32),
+        in_specs=[pl.BlockSpec(memory_space=pltpu.VMEM)] * 3,
+        out_specs=pl.BlockSpec(memory_space=pltpu.VMEM),
+        compiler_params=pltpu.CompilerParams(vmem_limit_bytes=VMEM_LIMIT),
+    )(own_sum, inverse_two, twin_inverse)
     return (a_update, b_update)
 
 

time: 161 us -> 155 us (0.963)
  the two profiles are of different devices: /device:TPU:17 before, /device:TPU:9 now
where the time goes in v1:
time: 155 us
  Pallas kernels  150 us (97%)
  local copies, waits for them, and re-layouts  2.42 us (2%)
  between operations  1.99 us (1%)
    pallas_call x3, Pallas kernels, remote_call(): pl.pallas_call(kernel, out_shape=[jax.ShapeDtypeStruct(shape, dtype) for...  101 us
    pallas_call x2, Pallas kernels, mode_call(): pl.pallas_call(kernel, grid_spec=grid_spec, out_shape=jax.ShapeDtypeStruc...  31.9 us
    pallas_call x2, Pallas kernels, inverse(): pl.pallas_call(inverse_kernel, out_shape=jax.ShapeDtypeStruct(gram.shape,...  14.6 us

profile of v1, /device:TPU:9, one launch (start us, length us, event | category | flops | bytes accessed | tf_op | source)
XLA Modules:
  0.0 154.7 jit_solution(11934719295519533082)
XLA Ops:
  1.3 0.6 broadcast_in_dim.9.n_ref
  1.9 32.9 %shard_map.86 = (bf16[2048,256]{1,0:T(8,128)(2,1)}, bf16[512,256]{1,0:T(8,128)(2,1)}, f32[256,256]{1,0:T(8,128)}, f32[256,256]{1,0:T(8,128)}, f32[8,128]{1,0:T(8,128)}) custom-call(f32[512,256]{1,0:T(8,128)} %b_ref.1, f32[128,256]{1,0:T(8,128)} %c_ref.1, f32[8,128]{1,0:T(8,128)} %broadcast_in_dim.9.n_ref), custom_call_target="tpu_custom_call" | custom-call | tf_op jit(solution)/shard_map/pallas_call | solution.py:485
  34.8 1.2 slice.3
  36.6 14.3 %shard_map.87.part_ref = f32[512,256]{1,0:T(8,128)} custom-call(s32[192]{0:T(256)} %i_ref.3, s32[192]{0:T(256)} %j_ref.3, s32[192]{0:T(256)} %k_ref.3, s32[1]{0:T(128)S(6)} %copy.10.n_ref, bf16[192,32,1024]{2,1,0:T(8,128)(2,1)} %x_ref.3, bf16[2048,256]{1,0:T(8,128)(2,1)} %get-tuple-element.12.b_ref, bf16[512,256]{1,0:T(8,128)(2,1)} %get-tuple-element.13.c_ref), custom_call_target="tpu_custom_call" | custom-call | flops 3221225472 | bytes 12582912 | tf_op jit(solution)/shard_map/pallas_call | solution.py:129
  50.9 7.8 %shard_map.88.inverse_ref = f32[256,256]{1,0:T(8,128)} custom-call(s32[1]{0:T(128)S(6)} %convert_element_type.18.lead_ref, f32[256,256]{1,0:T(8,128)} %get-tuple-element.15.g_ref), custom_call_target="tpu_custom_call" | custom-call | tf_op jit(solution)/shard_map/pallas_call | solution.py:203
  58.8 32.6 %shard_map.89 = (f32[64,256]{1,0:T(8,128)}, bf16[512,256]{1,0:T(8,128)(2,1)}, f32[256,256]{1,0:T(8,128)}) custom-call(f32[512,256]{1,0:T(8,128)} %shard_map.87.part_ref, f32[256,256]{1,0:T(8,128)} %shard_map.88.inverse_ref, f32[256,256]{1,0:T(8,128)} %get-tuple-element.16.third_ref), custom_call_target="tpu_custom_call" | custom-call | tf_op jit(solution)/shard_map/pallas_call | solution.py:485
  91.4 0.0 copy-start
  91.4 6.8 %shard_map.91.inverse_ref.mine_ref = f32[256,256]{1,0:T(8,128)} custom-call(s32[1]{0:T(128)S(6)} %convert_element_type.18.lead_ref, f32[256,256]{1,0:T(8,128)} %get-tuple-element.19.g_ref), custom_call_target="tpu_custom_call" | custom-call | tf_op jit(solution)/shard_map/pallas_call | solution.py:203
  98.2 17.6 %shard_map.90.part_ref = f32[2048,256]{1,0:T(8,128)} custom-call(s32[192]{0:T(256)} %i_ref.3, s32[192]{0:T(256)} %j_ref.3, s32[192]{0:T(256)} %k_ref.3, s32[1]{0:T(128)S(6)} %copy.10.n_ref, bf16[192,32,1024]{2,1,0:T(8,128)(2,1)} %x_ref.3, bf16[512,256]{1,0:T(8,128)(2,1)} %get-tuple-element.18.a_ref, bf16[512,256]{1,0:T(8,128)(2,1)} %get-tuple-element.13.c_ref), custom_call_target="tpu_custom_call" | custom-call | flops 3221225472 | bytes 12582912 | tf_op jit(solution)/shard_map/pallas_call | solution.py:129
  115.8 35.7 %shard_map.92 = (f32[512,256]{1,0:T(8,128)}, f32[256,256]{1,0:T(8,128)}) custom-call(f32[2048,256]{1,0:T(8,128)} %shard_map.90.part_ref, f32[256,256]{1,0:T(8,128)} %shard_map.91.inverse_ref.mine_ref), custom_call_target="tpu_custom_call" | custom-call | tf_op jit(solution)/shard_map/pallas_call | solution.py:485
  151.5 2.6 %shard_map.93 = f32[512,256]{1,0:T(8,128)} custom-call(f32[512,256]{1,0:T(8,128)} %get-tuple-element.20.sum_ref, f32[256,256]{1,0:T(8,128)} %shard_map.91.inverse_ref.mine_ref, f32[256,256]{1,0:T(8,128)} %get-tuple-element.21.other_ref), custom_call_target="tpu_custom_call" | custom-call | tf_op jit(solution)/shard_map/pallas_call | solution.py:573
  154.1 0.0 copy-done
  154.1 0.6 copy.11
Async XLA Ops:
  91.4 62.6 %copy-start = (f32[64,256]{1,0:T(8,128)S(1)}, f32[64,256]{1,0:T(8,128)}, u32[]{:S(2)}) copy-start(f32[64,256]{1,0:T(8,128)} %get-tuple-element.24) | copy-start | bytes 196612

commit v2 on v1

--- a/solution.py
+++ b/solution.py
@@ -7,8 +7,8 @@
 from jax.sharding import PartitionSpec as P
 
 HIGHEST = lax.Precision.HIGHEST
-GROUP = 16
-UNROLL = 8
+GROUP = 32
+UNROLL = 16
 QUARTER = 32
 LANES = 128
 VMEM_LIMIT = 56 * 1024 * 1024
@@ -351,6 +351,36 @@
     return dot(high, high) + (cross + cross.T)
 
 
+def gram_blocks(rank, grams, devices):
+    side = rank // LANES
+    upper = [(w, r, c) for w in range(grams) for r in range(side) for c in range(r, side)]
+    if len(upper) * LANES % (8 * devices) == 0:
+        return upper
+    return [(w, r, c) for w in range(grams) for r in range(side) for c in range(side)]
+
+
+def pack_gram(blocks, which, gram, ref):
+    for number, (w, r, c) in enumerate(blocks):
+        if w == which:
+            ref[number * LANES : (number + 1) * LANES, :] = gram[
+                r * LANES : (r + 1) * LANES, c * LANES : (c + 1) * LANES
+            ]
+
+
+def unpack_gram(blocks, which, ref):
+    found = {}
+    for number, (w, r, c) in enumerate(blocks):
+        if w == which:
+            found[r, c] = ref[number * LANES : (number + 1) * LANES, :]
+    for r, c in list(found):
+        if (c, r) not in found:
+            found[c, r] = found[r, c].T
+    side = max(r for r, _ in found) + 1
+    return jnp.concatenate(
+        [jnp.concatenate([found[r, c] for c in range(side)], axis=1) for r in range(side)], axis=0
+    )
+
+
 def gather_kernel(
     grp, col, b_ref, c_ref, n_ref, b_out, c_out, product_out, third_out, n_out,
     acc, landing, full, *sems,
@@ -367,20 +397,15 @@
         mine[...] = src[...].astype(jnp.bfloat16)
         for number, target in enumerate(others):
             pending.append(send(mine, mine, sems[2:], which * (grp - 1) + number, target))
-    for which, src in enumerate((b_ref, c_ref)):
-        gram = square(src[...])
-        for part in range(rank // LANES):
-            first = (which * (rank // LANES) + part) * rank
-            acc[first : first + rank, :] = gram[:, part * LANES : (part + 1) * LANES]
+    layout = gram_blocks(rank, 2, grp * col)
+    pack_gram(layout, 0, square(b_ref[...]), acc)
+    pack_gram(layout, 1, square(c_ref[...]), acc)
     offset, rows = scatter_all(groups, acc, landing, sems)
     full[rows_at(offset, rows), :] = acc[rows_at(offset, rows), :]
     spread_all(groups, full, sems, offset, rows)
-    half = acc.shape[0] // 2
-    for part in range(rank // LANES):
-        second = full[part * rank : (part + 1) * rank, :]
-        third = full[half + part * rank : half + (part + 1) * rank, :]
-        product_out[:, part * LANES : (part + 1) * LANES] = second * third
-        third_out[:, part * LANES : (part + 1) * LANES] = third
+    third = unpack_gram(layout, 1, full)
+    product_out[...] = unpack_gram(layout, 0, full) * third
+    third_out[...] = third
     for copy in pending:
         copy.wait()
 
@@ -390,7 +415,7 @@
     acc, landing, full, gram, piece, whole, other_inverse, *sems,
 ):
     g, c = me_of(grp)
-    total = part_ref.shape[0]
+    total, gram_rank = part_ref.shape
     own = total // col
     groups = [core_group(), chip_group(col)]
     others = targets_of([grp_group(grp)])
@@ -410,25 +435,13 @@
     update_out[...] = update
     full[rows_at(offset, rows), :] = update
     spread_all(groups, full, sems, offset, rows)
-    gram[...] = square(full[...])
-    size = gram.shape[0] // grp
-    copies = []
-    for number, target in enumerate(others):
-        copies.append(
-            send(gram.at[rows_at(target[0] * size, size), :], piece.at[number], sems[2:], number, target)
-        )
-    mine = gram[rows_at(g * size, size), :]
-    for number, copy in enumerate(copies):
-        copy.wait()
-        mine = mine + piece[number]
-    spot = whole.at[rows_at(g * size, size), :]
-    spot[...] = mine
-    copies = [
-        send(spot, spot, sems[2:], grp - 1 + number, target) for number, target in enumerate(others)
-    ]
-    for copy in copies:
-        copy.wait()
-    gram_first = whole[...]
+    layout = gram_blocks(gram_rank, 1, grp)
+    pack_gram(layout, 0, square(full[...]), gram)
+    groups = [grp_group(grp)]
+    offset, rows = scatter_all(groups, gram, piece, sems[2:])
+    whole[rows_at(offset, rows), :] = gram[rows_at(offset, rows), :]
+    spread_all(groups, whole, sems[2:], offset, rows)
+    gram_first = unpack_gram(layout, 0, whole)
     row = lax.broadcasted_iota(jnp.int32, gram_first.shape, 0)
     column = lax.broadcasted_iota(jnp.int32, gram_first.shape, 1)
     diagonal = jnp.where(row == column, gram_first, 0.0)
@@ -442,13 +455,11 @@
         ).astype(jnp.bfloat16)
 
 
-def second_factor_kernel(grp, part_ref, inverse_ref, out_ref, other_out, landing, *sems):
+def second_factor_kernel(grp, part_ref, out_ref, landing, *sems):
     g, c = me_of(grp)
     count = bits_of(grp)
     own = part_ref.shape[0] // grp
-    twin = core_group()[1][0][1]
-    greet([target for _, target in grp_stages(grp)] + [twin])
-    given = send(inverse_ref, other_out, sems[2:], 0, twin)
+    greet([target for _, target in grp_stages(grp)])
     half = part_ref.shape[1] // 2
     holding = []
     for h in range(2):
@@ -477,7 +488,6 @@
             del holding[h][m | (1 << bit)]
     for h in range(2):
         out_ref[:, h * half : (h + 1) * half] = holding[h][0][...]
-    given.wait()
 
 
 def remote_call(kernel, number, args, outs, scratch):
@@ -504,7 +514,8 @@
     grp, col = lax.axis_size("grp"), lax.axis_size("col")
     col_links = col // 2
     f32, bf16 = jnp.float32, jnp.bfloat16
-    gram_rows = 2 * rank * (rank // LANES)
+    gram_rows = len(gram_blocks(rank, 2, grp * col)) * LANES
+    first_gram = len(gram_blocks(rank, 1, grp)) * LANES
     b_range, c_range, gram_one, gram_third, twin_count = remote_call(
         functools.partial(gather_kernel, grp, col),
         0,
@@ -541,9 +552,9 @@
             pltpu.VMEM((first_rows, rank), f32),
             pltpu.VMEM((first_rows, rank), f32),
             pltpu.VMEM((first_rows, rank), f32),
-            pltpu.VMEM((rank, rank), f32),
-            pltpu.VMEM((grp - 1, rank // grp, rank), f32),
-            pltpu.VMEM((rank, rank), f32),
+            pltpu.VMEM((first_gram, LANES), f32),
+            pltpu.VMEM((first_gram, LANES), f32),
+            pltpu.VMEM((first_gram, LANES), f32),
             pltpu.VMEM((rank, rank), f32),
         ]
         + semaphores(2 * col_links)
@@ -551,6 +562,9 @@
         + semaphores(1),
     )
     inverse_two = inverse(lead, gram_two)
+    twin_inverse = lax.ppermute(
+        inverse_two, "col", [(c, c + 1 - 2 * (c % 2)) for c in range(col)]
+    )
     second_rows = b_range.shape[0]
     partial_two = mode_call(
         mode_two_kernel,
@@ -561,14 +575,13 @@
         second_rows,
         [pltpu.VMEM((UNROLL, 8 * edge, LANES), f32)],
     )
-    own_sum, twin_inverse = remote_call(
+    (own_sum,) = remote_call(
         functools.partial(second_factor_kernel, grp),
         2,
-        (partial_two, inverse_two),
-        [((second_rows // grp, rank), f32), ((rank, rank), f32)],
+        (partial_two,),
+        [((second_rows // grp, rank), f32)],
         [pltpu.VMEM((2, grp - 1, second_rows // grp, rank // 2), f32)]
-        + semaphores(2 * (grp - 1))
-        + semaphores(1),
+        + semaphores(2 * (grp - 1)),
     )
     b_update = pl.pallas_call(
         solve_kernel,

time: 155 us -> 147 us (0.948)
  Pallas kernels: 150 us -> 141 us
    pallas_call x2, Pallas kernels: 31.9 us -> 25.6 us  [mode_call(): pl.pallas_call(kernel, grid_spec=grid_spec, out_shape=jax.ShapeDtypeStruc...]
    pallas_call x3, Pallas kernels: 101 us -> 97.9 us  [remote_call(): pl.pallas_call(kernel, out_shape=[jax.ShapeDtypeStruct(shape, dtype) for...]
  transfers between devices with their start and end apart: 0 -> 1, of which waited for: 0 -> 0; matrix products, arithmetic and copies ran while one was open for 0% -> 0% of each run, Pallas kernels for 0% -> 33%
where the time goes in v2:
time: 147 us; the launch traced here: 146 us
  Pallas kernels  141 us (96%)
  local copies, waits for them, and re-layouts  3.11 us (2%)
  between operations  2.01 us (1%)
    pallas_call x3, Pallas kernels, remote_call(): pl.pallas_call(kernel, out_shape=[jax.ShapeDtypeStruct(shape, dtype) for...  97.9 us
    pallas_call x2, Pallas kernels, mode_call(): pl.pallas_call(kernel, grid_spec=grid_spec, out_shape=jax.ShapeDtypeStruc...  25.6 us
    pallas_call x2, Pallas kernels, inverse(): pl.pallas_call(inverse_kernel, out_shape=jax.ShapeDtypeStruct(gram.shape,...  14.6 us
  transfers between devices with their start and end apart: 1, of which 0 were waited for; matrix products, arithmetic and copies ran while one was open for 0% of the time, Pallas kernels for 33%

profile of v2, /device:TPU:9, one launch (start us, length us, event | category | flops | bytes accessed | tf_op | source)
XLA Modules:
  0.0 145.9 jit_solution(10101490403097807015)
XLA Ops:
  1.3 0.6 broadcast_in_dim.9.n_ref
  1.9 31.8 %shard_map.86 = (bf16[2048,256]{1,0:T(8,128)(2,1)}, bf16[512,256]{1,0:T(8,128)(2,1)}, f32[256,256]{1,0:T(8,128)}, f32[256,256]{1,0:T(8,128)}, f32[8,128]{1,0:T(8,128)}) custom-call(f32[512,256]{1,0:T(8,128)} %b_ref.1, f32[128,256]{1,0:T(8,128)} %c_ref.1, f32[8,128]{1,0:T(8,128)} %broadcast_in_dim.9.n_ref), custom_call_target="tpu_custom_call" | custom-call | tf_op jit(solution)/shard_map/pallas_call | solution.py:495
  33.6 1.2 slice.3
  35.5 7.9 %shard_map.88.inverse_ref = f32[256,256]{1,0:T(8,128)} custom-call(s32[1]{0:T(128)S(6)} %convert_element_type.18.lead_ref, f32[256,256]{1,0:T(8,128)} %get-tuple-element.13.g_ref), custom_call_target="tpu_custom_call" | custom-call | tf_op jit(solution)/shard_map/pallas_call | solution.py:203
  43.4 11.5 %shard_map.87.part_ref = f32[512,256]{1,0:T(8,128)} custom-call(s32[192]{0:T(256)} %i_ref.3, s32[192]{0:T(256)} %j_ref.3, s32[192]{0:T(256)} %k_ref.3, s32[1]{0:T(128)S(6)} %copy.10.n_ref, bf16[192,32,1024]{2,1,0:T(8,128)(2,1)} %x_ref.3, bf16[2048,256]{1,0:T(8,128)(2,1)} %get-tuple-element.10.b_ref, bf16[512,256]{1,0:T(8,128)(2,1)} %get-tuple-element.11.c_ref), custom_call_target="tpu_custom_call" | custom-call | flops 3221225472 | bytes 12582912 | tf_op jit(solution)/shard_map/pallas_call | solution.py:129
  54.8 32.8 %shard_map.89 = (f32[64,256]{1,0:T(8,128)}, bf16[512,256]{1,0:T(8,128)(2,1)}, f32[256,256]{1,0:T(8,128)}) custom-call(f32[512,256]{1,0:T(8,128)} %shard_map.87.part_ref, f32[256,256]{1,0:T(8,128)} %shard_map.88.inverse_ref, f32[256,256]{1,0:T(8,128)} %get-tuple-element.14.third_ref), custom_call_target="tpu_custom_call" | custom-call | tf_op jit(solution)/shard_map/pallas_call | solution.py:495
  87.6 0.0 copy-start.1
  87.6 6.8 %shard_map.92.mine_ref = f32[256,256]{1,0:T(8,128)} custom-call(s32[1]{0:T(128)S(6)} %convert_element_type.18.lead_ref, f32[256,256]{1,0:T(8,128)} %get-tuple-element.17.g_ref), custom_call_target="tpu_custom_call" | custom-call | tf_op jit(solution)/shard_map/pallas_call | solution.py:203
  94.4 0.0 collective-permute-start
  94.4 14.2 %shard_map.90.part_ref = f32[2048,256]{1,0:T(8,128)} custom-call(s32[192]{0:T(256)} %i_ref.3, s32[192]{0:T(256)} %j_ref.3, s32[192]{0:T(256)} %k_ref.3, s32[1]{0:T(128)S(6)} %copy.10.n_ref, bf16[192,32,1024]{2,1,0:T(8,128)(2,1)} %x_ref.3, bf16[512,256]{1,0:T(8,128)(2,1)} %get-tuple-element.16.a_ref, bf16[512,256]{1,0:T(8,128)(2,1)} %get-tuple-element.11.c_ref), custom_call_target="tpu_custom_call" | custom-call | flops 3221225472 | bytes 12582912 | tf_op jit(solution)/shard_map/pallas_call | solution.py:129
  108.6 33.4 %shard_map.91.sum_ref = f32[512,256]{1,0:T(8,128)} custom-call(f32[2048,256]{1,0:T(8,128)} %shard_map.90.part_ref), custom_call_target="tpu_custom_call" | custom-call | tf_op jit(solution)/shard_map/pallas_call | solution.py:495
  142.0 0.0 collective-permute-done.other_ref
  142.0 0.0 copy-start
  142.0 0.7 copy-done
  142.7 2.6 %shard_map.93 = f32[512,256]{1,0:T(8,128)} custom-call(f32[512,256]{1,0:T(8,128)} %shard_map.91.sum_ref, f32[256,256]{1,0:T(8,128)} %shard_map.92.mine_ref, f32[256,256]{1,0:T(8,128)} %copy-done), custom_call_target="tpu_custom_call" | custom-call | tf_op jit(solution)/shard_map/pallas_call | solution.py:586
  145.3 0.0 copy-done.1
  145.3 0.6 copy.11
Async XLA Ops:
  87.6 57.6 %copy-start.1 = (f32[64,256]{1,0:T(8,128)S(1)}, f32[64,256]{1,0:T(8,128)}, u32[]{:S(2)}) copy-start(f32[64,256]{1,0:T(8,128)} %get-tuple-element.20) | copy-start | bytes 196612
  94.4 47.6 %collective-permute-start = (f32[256,256]{1,0:T(8,128)}, f32[256,256]{1,0:T(8,128)S(1)}, u32[]{:S(2)}, u32[]{:S(2)}) collective-permute-start(f32[256,256]{1,0:T(8,128)} %shard_map.92.mine_ref), channel_id=1, source_target_pairs={{0,1},{1,0},{2,3},{3,2},{4,5},{5,4},{6,7},{7,6},{8,9},{9,8},{10,11... | collective-permute-start | bytes 786440 | tf_op jit(solution)/shard_map/ppermute | solution.py:565
  142.0 0.7 copy-start
